TPU v7x, 512 devices: a whole 4x8x8 slice. The times are simulated.
512 devices in a mesh: grp: 16 (over x, z_hi), body: 32 (over y, z_lo, core).
Axes of the slice: x: 4, y: 8, z: 8 (z_hi: 4, z_lo: 2; z = z_hi * 2 + z_lo), core: 2. Of those that a mesh axis runs over, the one named last changes fastest.
Arguments:
- incident: bfloat16 [512, 16, 512], P(('grp', 'body')), may hold values from -6 to 6
- exciting: float32 [512, 16, 512], P(('grp', 'body')), may hold values from -6 to 6
- t_matrices: bfloat16 [512, 2, 256, 256], P(('grp', 'body')), may hold values from -0.1875 to 0.1875
- hankel_rows: bfloat16 [225, 2, 512], replicated, may hold values from -0.046875 to 0.046875
- offsets: int32 [512, 32], P(('grp', 'body')), may hold values from 0 to 224
- lattice_slots: int32 [512], P('grp'), may hold values from 0 to 31, as said below
- up_maps: bfloat16 [512, 2, 256, 512], P(('grp', 'body')), may hold values from -0.0625 to 0.0625
- down_maps: bfloat16 [512, 2, 512, 256], P(('grp', 'body')), may hold values from -0.1875 to 0.1875
- group_maps: bfloat16 [16, 16, 2, 512, 512], P('grp', None, None, 'body'), may hold values from -0.046875 to 0.046875
Outputs:
- updated: float32 [512, 16, 512], P(('grp', 'body'))
Inputs may be any that keep to these rules, and one draw needn't show every extreme that they name: `lattice_slots`: within each group the 32 columns stand at the slots 0 to 31, one column a slot.
All inputs are finite; a program needn't handle non-finite values.
Results may differ from a plain program's by a relative error of at most 0.0034.
Values may be sent and summed in bfloat16 or wider, within the bound.
A program may use at most 64 MiB of HBM per device.

v0:
```python
import math
import jax
import jax.numpy as jnp
from jax import lax
from jax.sharding import PartitionSpec as P


def complex_apply(form, values, real_mats, imag_mats):
    half_width = values.shape[-1] // 2
    real_values = values[..., :half_width]
    imag_values = values[..., half_width:]
    real_out = jnp.einsum(
        form, real_values, real_mats, preferred_element_type=jnp.float32
    ) - jnp.einsum(form, imag_values, imag_mats, preferred_element_type=jnp.float32)
    imag_out = jnp.einsum(
        form, real_values, imag_mats, preferred_element_type=jnp.float32
    ) + jnp.einsum(form, imag_values, real_mats, preferred_element_type=jnp.float32)
    return jnp.concatenate([real_out, imag_out], axis=-1)


def toeplitz_mats(sequences):
    length = sequences.shape[-1] // 2
    repeats = (1,) * (sequences.ndim - 1) + (length,)
    tiled = jnp.tile(sequences, repeats)
    window = tiled[..., length : length + length * (2 * length - 1)]
    return window.reshape(sequences.shape[:-1] + (length, 2 * length - 1))[..., :length]


def local(
    incident,
    exciting,
    t_matrices,
    hankel_rows,
    offsets,
    lattice_slots,
    up_maps,
    down_maps,
    group_maps,
):
    body_index = lax.axis_index("body")
    group_index = lax.axis_index("grp")
    local_count = incident.shape[0]
    scattered = complex_apply("iln,inm->ilm", incident, t_matrices[:, 0], t_matrices[:, 1]).astype(
        jnp.bfloat16
    )
    own_members = body_index * local_count + jnp.arange(local_count, dtype=jnp.int32)
    zero_seq = jnp.zeros((), jnp.bfloat16)
    all_offsets = lax.all_gather(offsets, "body", axis=0, tiled=True)
    group_count = lattice_slots.shape[0]
    own_slots = lax.dynamic_slice_in_dim(lattice_slots, body_index * local_count, local_count, 0)
    table_rows = jnp.take(all_offsets, own_slots, axis=1)
    sequences = jnp.take(hankel_rows, table_rows, axis=0)
    targets = jnp.arange(group_count, dtype=jnp.int32)
    keep = targets[:, None] != own_members[None, :]
    sequences = jnp.where(keep[:, :, None, None], sequences, zero_seq)
    block_rows = math.gcd(group_count, 4)
    sequences = sequences.reshape((group_count // block_rows, block_rows) + sequences.shape[1:])

    def one_block(block_seqs):
        mats = toeplitz_mats(block_seqs)
        return complex_apply("sln,tsnm->tlm", scattered, mats[:, :, 0], mats[:, :, 1])

    terms = lax.map(one_block, sequences)
    totals = lax.psum(terms.reshape((group_count,) + terms.shape[2:]), "body")
    near = lax.dynamic_slice_in_dim(totals, body_index * local_count, local_count, 0)
    partial_value = complex_apply("iln,inq->lq", scattered, up_maps[:, 0], up_maps[:, 1])
    expansion = lax.psum(partial_value, "body").astype(jnp.bfloat16)
    block_width = group_maps.shape[3]
    full_width = group_maps.shape[4]
    real_block = lax.dynamic_slice_in_dim(expansion, body_index * block_width, block_width, 1)
    imag_block = lax.dynamic_slice_in_dim(
        expansion, full_width + body_index * block_width, block_width, 1
    )
    own_block = jnp.concatenate([real_block, imag_block], axis=-1)[None]
    piece = lax.all_gather(own_block, "grp", axis=0, tiled=True)
    width = piece.shape[0]
    sources = jnp.arange(width, dtype=jnp.int32)
    piece = jnp.where((sources != group_index)[:, None, None], piece, zero_seq)
    mats = group_maps[0]
    incoming_part = complex_apply("hln,hnq->lq", piece, mats[:, 0], mats[:, 1])
    incoming = lax.psum(incoming_part, "body").astype(jnp.bfloat16)
    far = complex_apply("lq,iqp->ilp", incoming, down_maps[:, 0], down_maps[:, 1])
    return exciting + near + far


def solution(mesh):
    return jax.shard_map(
        local,
        mesh=mesh,
        in_specs=(
            P(("grp", "body"), None, None),
            P(("grp", "body"), None, None),
            P(("grp", "body"), None, None, None),
            P(),
            P(("grp", "body"), None),
            P("grp"),
            P(("grp", "body"), None, None, None),
            P(("grp", "body"), None, None, None),
            P("grp", None, None, "body", None),
        ),
        out_specs=P(("grp", "body"), None, None),
        check_vma=False,
    )
```

profile of v0, /device:TPU:32, one launch (start us, length us, event | category | flops | bytes accessed | tf_op | source)
XLA Modules:
  0.0 437.4 jit_solution(12570242964982283185)
XLA Ops:
  8.7 1.3 dynamic_slice.16
  12.1 32.7 %all-gather.1 = s32[32,1,32]{2,1,0:T(1,128)S(1)} all-gather(s32[1,1,32]{2,1,0:T(1,128)} %bitcast.159), channel_id=1, replica_groups=mesh['grp'=16,'body'=32] {'body'}, dimensions={0}, use_global_device_ids=true | all-gather | bytes 4224 | tf_op jit(solution)/shard_map/all_gather | solution.py:48
  44.8 1.3 fusion.67
  49.3 119.1 %while.11 = (s32[]{:T(128)}, f32[8,4,16,512]{3,2,1,0:T(8,128)}, bf16[8,4,1,2,512]{4,3,1,2,0:T(2,128)(2,1)S(1)}, bf16[1,16,512]{2,1,0:T(8,128)(2,1)S(1)}, s32[]{:T(128)}) while((s32[]{:T(128)}, f32[8,4,16,512]{3,2,1,0:T(8,128)}, bf16[8,4,1,2,512]{4,3,1,2,0:T(2,128)(2,1)S(1)}, bf16[1,16,512]{2,1,0:T(8,128)(2,1)S(1)}, s32[]{:T(128)}) %tuple.28), condition=%wide.region_1.2_spmd, body=%wide.region_0.1_spmd.sunk | while | flops 33619968 | bytes 17474112 | solution.py:63
  49.5 2.8 tile.14
  52.3 4.4 %slice.219 = bf16[4,1,2,130816]{3,2,0,1:T(2,128)(2,1)} slice(bf16[4,1,2,131072]{3,2,0,1:T(2,128)(2,1)} %tile.14), slice={[0:4], [0:1], [0:2], [256:131072]} | slice | bytes 4186112 | tf_op jit(solution)/shard_map/while/body/eval_jaxpr/slice | solution.py:25
  56.7 6.1 %reshape.288 = bf16[4,1,2,256,511]{4,3,2,0,1:T(8,128)(2,1)S(1)} reshape(bf16[4,1,2,130816]{3,2,0,1:T(2,128)(2,1)} %slice.219) | data formatting | bytes 4186112 | tf_op jit(solution)/shard_map/while/body/eval_jaxpr/reshape | solution.py:26
  64.4 2.8 tile.14
  67.2 4.4 %slice.219 = bf16[4,1,2,130816]{3,2,0,1:T(2,128)(2,1)} slice(bf16[4,1,2,131072]{3,2,0,1:T(2,128)(2,1)} %tile.14), slice={[0:4], [0:1], [0:2], [256:131072]} | slice | bytes 4186112 | tf_op jit(solution)/shard_map/while/body/eval_jaxpr/slice | solution.py:25
  71.6 6.1 %reshape.288 = bf16[4,1,2,256,511]{4,3,2,0,1:T(8,128)(2,1)S(1)} reshape(bf16[4,1,2,130816]{3,2,0,1:T(2,128)(2,1)} %slice.219) | data formatting | bytes 4186112 | tf_op jit(solution)/shard_map/while/body/eval_jaxpr/reshape | solution.py:26
  79.2 2.8 tile.14
  82.0 4.4 %slice.219 = bf16[4,1,2,130816]{3,2,0,1:T(2,128)(2,1)} slice(bf16[4,1,2,131072]{3,2,0,1:T(2,128)(2,1)} %tile.14), slice={[0:4], [0:1], [0:2], [256:131072]} | slice | bytes 4186112 | tf_op jit(solution)/shard_map/while/body/eval_jaxpr/slice | solution.py:25
  86.4 6.1 %reshape.288 = bf16[4,1,2,256,511]{4,3,2,0,1:T(8,128)(2,1)S(1)} reshape(bf16[4,1,2,130816]{3,2,0,1:T(2,128)(2,1)} %slice.219) | data formatting | bytes 4186112 | tf_op jit(solution)/shard_map/while/body/eval_jaxpr/reshape | solution.py:26
  94.1 2.8 tile.14
  96.9 4.4 %slice.219 = bf16[4,1,2,130816]{3,2,0,1:T(2,128)(2,1)} slice(bf16[4,1,2,131072]{3,2,0,1:T(2,128)(2,1)} %tile.14), slice={[0:4], [0:1], [0:2], [256:131072]} | slice | bytes 4186112 | tf_op jit(solution)/shard_map/while/body/eval_jaxpr/slice | solution.py:25
  101.3 6.1 %reshape.288 = bf16[4,1,2,256,511]{4,3,2,0,1:T(8,128)(2,1)S(1)} reshape(bf16[4,1,2,130816]{3,2,0,1:T(2,128)(2,1)} %slice.219) | data formatting | bytes 4186112 | tf_op jit(solution)/shard_map/while/body/eval_jaxpr/reshape | solution.py:26
  109.0 2.8 tile.14
  111.8 4.4 %slice.219 = bf16[4,1,2,130816]{3,2,0,1:T(2,128)(2,1)} slice(bf16[4,1,2,131072]{3,2,0,1:T(2,128)(2,1)} %tile.14), slice={[0:4], [0:1], [0:2], [256:131072]} | slice | bytes 4186112 | tf_op jit(solution)/shard_map/while/body/eval_jaxpr/slice | solution.py:25
  116.2 6.1 %reshape.288 = bf16[4,1,2,256,511]{4,3,2,0,1:T(8,128)(2,1)S(1)} reshape(bf16[4,1,2,130816]{3,2,0,1:T(2,128)(2,1)} %slice.219) | data formatting | bytes 4186112 | tf_op jit(solution)/shard_map/while/body/eval_jaxpr/reshape | solution.py:26
  123.9 2.8 tile.14
  126.7 4.4 %slice.219 = bf16[4,1,2,130816]{3,2,0,1:T(2,128)(2,1)} slice(bf16[4,1,2,131072]{3,2,0,1:T(2,128)(2,1)} %tile.14), slice={[0:4], [0:1], [0:2], [256:131072]} | slice | bytes 4186112 | tf_op jit(solution)/shard_map/while/body/eval_jaxpr/slice | solution.py:25
  131.1 6.1 %reshape.288 = bf16[4,1,2,256,511]{4,3,2,0,1:T(8,128)(2,1)S(1)} reshape(bf16[4,1,2,130816]{3,2,0,1:T(2,128)(2,1)} %slice.219) | data formatting | bytes 4186112 | tf_op jit(solution)/shard_map/while/body/eval_jaxpr/reshape | solution.py:26
  138.8 2.8 tile.14
  141.6 4.4 %slice.219 = bf16[4,1,2,130816]{3,2,0,1:T(2,128)(2,1)} slice(bf16[4,1,2,131072]{3,2,0,1:T(2,128)(2,1)} %tile.14), slice={[0:4], [0:1], [0:2], [256:131072]} | slice | bytes 4186112 | tf_op jit(solution)/shard_map/while/body/eval_jaxpr/slice | solution.py:25
  146.0 6.1 %reshape.288 = bf16[4,1,2,256,511]{4,3,2,0,1:T(8,128)(2,1)S(1)} reshape(bf16[4,1,2,130816]{3,2,0,1:T(2,128)(2,1)} %slice.219) | data formatting | bytes 4186112 | tf_op jit(solution)/shard_map/while/body/eval_jaxpr/reshape | solution.py:26
  153.6 2.8 tile.14
  156.4 4.4 %slice.219 = bf16[4,1,2,130816]{3,2,0,1:T(2,128)(2,1)} slice(bf16[4,1,2,131072]{3,2,0,1:T(2,128)(2,1)} %tile.14), slice={[0:4], [0:1], [0:2], [256:131072]} | slice | bytes 4186112 | tf_op jit(solution)/shard_map/while/body/eval_jaxpr/slice | solution.py:25
  160.8 6.1 %reshape.288 = bf16[4,1,2,256,511]{4,3,2,0,1:T(8,128)(2,1)S(1)} reshape(bf16[4,1,2,130816]{3,2,0,1:T(2,128)(2,1)} %slice.219) | data formatting | bytes 4186112 | tf_op jit(solution)/shard_map/while/body/eval_jaxpr/reshape | solution.py:26
  169.0 104.8 %psum.22 = bf16[16,1024]{1,0:T(8,128)(2,1)S(1)} all-reduce(f32[16,1024]{1,0:T(8,128)S(1)} %pad_maximum_fusion), channel_id=1, replica_groups=mesh['grp'=16,'body'=32] {'body'}, use_global_device_ids=true, to_apply=%region_3.4 | all-reduce | flops 16384 | bytes 98304 | tf_op jit(solution)/shard_map/psum | solution.py:67
  274.0 48.7 %all-gather = bf16[256,32]{1,0:T(8,128)(2,1)S(1)} all-gather(bf16[16,32]{1,0:T(8,128)(2,1)S(1)} %pad_maximum_fusion.3), channel_id=2, replica_groups=mesh['grp'=16,'body'=32] {'grp'}, dimensions={0}, use_global_device_ids=true | all-gather | bytes 17408 | tf_op jit(solution)/shard_map/all_gather | solution.py:75
  324.0 104.5 %psum.23 = bf16[16,1024]{1,0:T(8,128)(2,1)S(1)} all-reduce(f32[16,1024]{1,0:T(8,128)S(1)} %pad_maximum_fusion.1), channel_id=1, replica_groups=mesh['grp'=16,'body'=32] {'body'}, use_global_device_ids=true, to_apply=%region_4.5 | all-reduce | flops 16384 | bytes 98304 | tf_op jit(solution)/shard_map/psum | solution.py:81
  429.2 1.4 maximum_add_fusion
  (99 shorter events, 20.5 us)
Async XLA Ops:
  6.5 41.9 %copy-start = (bf16[225,2,512]{2,1,0:T(2,128)(2,1)S(1)}, bf16[225,2,512]{2,1,0:T(2,128)(2,1)}, u32[]{:S(2)}) copy-start(bf16[225,2,512]{2,1,0:T(2,128)(2,1)} %param.14) | copy-start | bytes 1382404
  6.5 422.6 %all-reduce.2.cloned.1.call-start = ((), (), s32[]{:S(2)}) async-start(), calls=%async_computation | async-start | bytes 2097152 | tf_op jit(solution)/shard_map/psum | solution.py:64
  49.3 119.1 %copy-start.2 = (bf16[1,2,256,512]{3,2,1,0:T(8,128)(2,1)S(1)}, bf16[1,2,256,512]{3,2,1,0:T(8,128)(2,1)}, u32[]{:S(2)}) copy-start(bf16[1,2,256,512]{3,2,1,0:T(8,128)(2,1)} %param.17) | copy-start | bytes 1572868
  168.4 154.4 %copy-start.3 = (bf16[1,16,2,16,512]{4,3,2,1,0:T(8,128)(2,1)S(1)}, bf16[1,16,2,16,512]{4,3,2,1,0:T(8,128)(2,1)}, u32[]{:S(2)}) copy-start(bf16[1,16,2,16,512]{4,3,2,1,0:T(8,128)(2,1)} %param.19) | copy-start | bytes 1572868
  168.7 259.9 %copy-start.1 = (bf16[1,2,512,256]{3,2,1,0:T(8,128)(2,1)S(1)}, bf16[1,2,512,256]{3,2,1,0:T(8,128)(2,1)}, u32[]{:S(2)}) copy-start(bf16[1,2,512,256]{3,2,1,0:T(8,128)(2,1)} %param.18) | copy-start | bytes 1572868
  322.7 106.4 %copy-start.4 = (f32[1,16,512]{2,1,0:T(8,128)S(1)}, f32[1,16,512]{2,1,0:T(8,128)}, u32[]{:S(2)}) copy-start(f32[1,16,512]{2,1,0:T(8,128)} %param.12) | copy-start | bytes 98308
Sparse Core Ops, SparseCore 0:
  168.5 234.8 all-reduce.1
where the time goes:
time: 438 us; the launch traced here: 437 us
  blocking collectives  291 us (66%)
  local copies, waits for them, and re-layouts  110 us (25%)
  between operations  15.6 us (4%)
  matrix products  12.5 us (3%)
  other arithmetic  8.4 us (2%)
    psum x1, blocking collectives, local(): expansion = lax.psum(partial_value, 'body').astype(jnp.bfloat16)  105 us
    psum x1, blocking collectives, local(): incoming = lax.psum(incoming_part, 'body').astype(jnp.bfloat16)  105 us
    all_gather x1, blocking collectives, local(): piece = lax.all_gather(own_block, 'grp', axis=0, tiled=True)  48.7 us
    reshape x8, local copies, waits for them, and re-layouts, toeplitz_mats(): window.reshape(sequences.shape[:-1] + (length, 2 * length - 1))  48.7 us
    slice x8, local copies, waits for them, and re-layouts, toeplitz_mats(): window = tiled[..., length:length + length * (2 * length - 1)]  35.2 us
    all_gather x1, blocking collectives, local(): all_offsets = lax.all_gather(offsets, 'body', axis=0, tiled=True)  32.7 us
    another operation x24, local copies, waits for them, and re-layouts, toeplitz_mats(): tiled = jnp.tile(sequences, repeats)  23.8 us
  transfers between devices with their start and end apart: 1, of which 0 were waited for; matrix products, arithmetic and copies ran while one was open for 1% of the time, Pallas kernels for 0%

commit v1 on v0

--- a/solution.py
+++ b/solution.py
@@ -45,7 +45,9 @@
     )
     own_members = body_index * local_count + jnp.arange(local_count, dtype=jnp.int32)
     zero_seq = jnp.zeros((), jnp.bfloat16)
-    all_offsets = lax.all_gather(offsets, "body", axis=0, tiled=True)
+    all_offsets = jnp.concatenate(
+        lax.all_to_all(jnp.stack([offsets] * lax.axis_size("body")), "body", 0, 0), axis=0
+    )
     group_count = lattice_slots.shape[0]
     own_slots = lax.dynamic_slice_in_dim(lattice_slots, body_index * local_count, local_count, 0)
     table_rows = jnp.take(all_offsets, own_slots, axis=1)

time: 438 us -> 541 us (1.24)
  the two profiles are of different devices: /device:TPU:32 before, /device:TPU:1 now
where the time goes in v1:
time: 541 us; the launch traced here: 540 us
  blocking collectives  257 us (48%)
  waiting for transfers between devices  121 us (22%)
  local copies, waits for them, and re-layouts  110 us (20%)
  matrix products  17.2 us (3%)
  between operations  15.4 us (3%)
  starting transfers between devices  10.6 us (2%)
  other arithmetic  8.46 us (2%)
    psum x1, waiting for transfers between devices, local(): totals = lax.psum(terms.reshape((group_count,) + terms.shape[2:]), 'body')  121 us
    psum x1, blocking collectives, local(): incoming = lax.psum(incoming_part, 'body').astype(jnp.bfloat16)  112 us
    psum x1, blocking collectives, local(): expansion = lax.psum(partial_value, 'body').astype(jnp.bfloat16)  104 us
    reshape x8, local copies, waits for them, and re-layouts, toeplitz_mats(): window.reshape(sequences.shape[:-1] + (length, 2 * length - 1))  48.7 us
    all_gather x1, blocking collectives, local(): piece = lax.all_gather(own_block, 'grp', axis=0, tiled=True)  41.5 us
    slice x8, local copies, waits for them, and re-layouts, toeplitz_mats(): window = tiled[..., length:length + length * (2 * length - 1)]  34.6 us
    another operation x24, local copies, waits for them, and re-layouts, toeplitz_mats(): tiled = jnp.tile(sequences, repeats)  23.7 us
  transfers between devices with their start and end apart: 2, of which 1 were waited for; matrix products, arithmetic and copies ran while one was open for 2% of the time, Pallas kernels for 0%

profile of v1, /device:TPU:1, one launch (start us, length us, event | category | flops | bytes accessed | tf_op | source)
XLA Modules:
  0.0 539.6 jit_solution(1764532134577253470)
XLA Ops:
  6.5 1.4 stack.2
  7.9 10.6 %all-to-all-start = ((s32[32,1,32]{2,1,0:T(1,128)}), s32[32,1,32]{2,1,0:T(1,128)S(1)}, u32[]{:S(2)}, u32[]{:S(2)}) async-start(s32[32,1,32]{2,1,0:T(1,128)} %stack.2), calls=%async_computation | async-start | bytes 32768 | tf_op jit(solution)/shard_map/all_to_all | solution.py:49
  27.2 103.9 %psum.22 = bf16[16,1024]{1,0:T(8,128)(2,1)S(1)} all-reduce(f32[16,1024]{1,0:T(8,128)S(1)} %pad_maximum_fusion), channel_id=1, replica_groups=mesh['grp'=16,'body'=32] {'body'}, use_global_device_ids=true, to_apply=%region_3.4 | all-reduce | flops 16384 | bytes 98304 | tf_op jit(solution)/shard_map/psum | solution.py:69
  131.3 41.5 %all-gather = bf16[256,32]{1,0:T(8,128)(2,1)S(1)} all-gather(bf16[16,32]{1,0:T(8,128)(2,1)S(1)} %pad_maximum_fusion.3), channel_id=2, replica_groups=mesh['grp'=16,'body'=32] {'grp'}, dimensions={0}, use_global_device_ids=true | all-gather | bytes 17408 | tf_op jit(solution)/shard_map/all_gather | solution.py:77
  178.7 118.5 %while.11 = (s32[]{:T(128)}, f32[8,4,16,512]{3,2,1,0:T(8,128)}, bf16[8,4,1,2,512]{4,3,1,2,0:T(2,128)(2,1)S(1)}, bf16[1,16,512]{2,1,0:T(8,128)(2,1)S(1)}, s32[]{:T(128)}) while((s32[]{:T(128)}, f32[8,4,16,512]{3,2,1,0:T(8,128)}, bf16[8,4,1,2,512]{4,3,1,2,0:T(2,128)(2,1)S(1)}, bf16[1,16,512]{2,1,0:T(8,128)(2,1)S(1)}, s32[]{:T(128)}) %tuple.29), condition=%wide.region_1.2_spmd, body=%wide.region_0.1_spmd.sunk | while | flops 33619968 | bytes 17474112 | solution.py:65
  178.9 2.8 tile.14
  181.7 4.3 slice.219
  186.0 6.1 %reshape.289 = bf16[4,1,2,256,511]{4,3,2,0,1:T(8,128)(2,1)S(1)} reshape(bf16[4,1,2,130816]{3,2,0,1:T(2,128)(2,1)} %slice.219) | data formatting | bytes 4186112 | tf_op jit(solution)/shard_map/while/body/eval_jaxpr/reshape | solution.py:26
  193.7 2.8 tile.14
  196.5 4.3 slice.219
  200.8 6.1 %reshape.289 = bf16[4,1,2,256,511]{4,3,2,0,1:T(8,128)(2,1)S(1)} reshape(bf16[4,1,2,130816]{3,2,0,1:T(2,128)(2,1)} %slice.219) | data formatting | bytes 4186112 | tf_op jit(solution)/shard_map/while/body/eval_jaxpr/reshape | solution.py:26
  208.5 2.8 tile.14
  211.3 4.3 slice.219
  215.6 6.1 %reshape.289 = bf16[4,1,2,256,511]{4,3,2,0,1:T(8,128)(2,1)S(1)} reshape(bf16[4,1,2,130816]{3,2,0,1:T(2,128)(2,1)} %slice.219) | data formatting | bytes 4186112 | tf_op jit(solution)/shard_map/while/body/eval_jaxpr/reshape | solution.py:26
  223.3 2.8 tile.14
  226.1 4.3 slice.219
  230.5 6.1 %reshape.289 = bf16[4,1,2,256,511]{4,3,2,0,1:T(8,128)(2,1)S(1)} reshape(bf16[4,1,2,130816]{3,2,0,1:T(2,128)(2,1)} %slice.219) | data formatting | bytes 4186112 | tf_op jit(solution)/shard_map/while/body/eval_jaxpr/reshape | solution.py:26
  238.1 2.8 tile.14
  240.9 4.3 slice.219
  245.3 6.1 %reshape.289 = bf16[4,1,2,256,511]{4,3,2,0,1:T(8,128)(2,1)S(1)} reshape(bf16[4,1,2,130816]{3,2,0,1:T(2,128)(2,1)} %slice.219) | data formatting | bytes 4186112 | tf_op jit(solution)/shard_map/while/body/eval_jaxpr/reshape | solution.py:26
  253.0 2.8 tile.14
  255.8 4.3 slice.219
  260.1 6.1 %reshape.289 = bf16[4,1,2,256,511]{4,3,2,0,1:T(8,128)(2,1)S(1)} reshape(bf16[4,1,2,130816]{3,2,0,1:T(2,128)(2,1)} %slice.219) | data formatting | bytes 4186112 | tf_op jit(solution)/shard_map/while/body/eval_jaxpr/reshape | solution.py:26
  267.8 2.8 tile.14
  270.6 4.3 slice.219
  274.9 6.1 %reshape.289 = bf16[4,1,2,256,511]{4,3,2,0,1:T(8,128)(2,1)S(1)} reshape(bf16[4,1,2,130816]{3,2,0,1:T(2,128)(2,1)} %slice.219) | data formatting | bytes 4186112 | tf_op jit(solution)/shard_map/while/body/eval_jaxpr/reshape | solution.py:26
  282.6 2.8 tile.14
  285.4 4.3 slice.219
  289.7 6.1 %reshape.289 = bf16[4,1,2,256,511]{4,3,2,0,1:T(8,128)(2,1)S(1)} reshape(bf16[4,1,2,130816]{3,2,0,1:T(2,128)(2,1)} %slice.219) | data formatting | bytes 4186112 | tf_op jit(solution)/shard_map/while/body/eval_jaxpr/reshape | solution.py:26
  298.4 111.7 %psum.23 = bf16[16,1024]{1,0:T(8,128)(2,1)S(1)} all-reduce(f32[16,1024]{1,0:T(8,128)S(1)} %pad_maximum_fusion.1), channel_id=1, replica_groups=mesh['grp'=16,'body'=32] {'body'}, use_global_device_ids=true, to_apply=%region_4.5 | all-reduce | flops 16384 | bytes 98304 | tf_op jit(solution)/shard_map/psum | solution.py:83
  410.7 120.6 %all-reduce.2.cloned.1.call-done = f32[32,16,512]{2,1,0:T(8,128)} async-done(((f32[32,16,512]{2,1,0:T(8,128)}), f32[32,16,512]{2,1,0:T(8,128)}) %all-reduce.2.cloned.1.call-update) | async-done | bytes 1048592 | tf_op jit(solution)/shard_map/psum | solution.py:66
  531.4 1.4 maximum_add_fusion
  (103 shorter events, 27.2 us)
Async XLA Ops:
  6.5 171.3 %copy-start = (bf16[225,2,512]{2,1,0:T(2,128)(2,1)S(1)}, bf16[225,2,512]{2,1,0:T(2,128)(2,1)}, u32[]{:S(2)}) copy-start(bf16[225,2,512]{2,1,0:T(2,128)(2,1)} %param.14) | copy-start | bytes 1382404
  6.5 166.3 %copy-start.2 = (bf16[1,16,2,16,512]{4,3,2,1,0:T(8,128)(2,1)S(1)}, bf16[1,16,2,16,512]{4,3,2,1,0:T(8,128)(2,1)}, u32[]{:S(2)}) copy-start(bf16[1,16,2,16,512]{4,3,2,1,0:T(8,128)(2,1)} %param.19) | copy-start | bytes 1572868
  7.9 168.5 %all-to-all-start = ((s32[32,1,32]{2,1,0:T(1,128)}), s32[32,1,32]{2,1,0:T(1,128)S(1)}, u32[]{:S(2)}, u32[]{:S(2)}) async-start(s32[32,1,32]{2,1,0:T(1,128)} %stack.2), calls=%async_computation | async-start | bytes 32768 | tf_op jit(solution)/shard_map/all_to_all | solution.py:49
  18.5 512.9 %all-reduce.2.cloned.1.call-start = ((), (), s32[]{:S(2)}) async-start(), calls=%async_computation.1 | async-start | bytes 2097152 | tf_op jit(solution)/shard_map/psum | solution.py:66
  22.8 151.0 %copy-start.5 = (s32[32]{0:T(128)S(1)}, s32[32]{0:T(128)}, u32[]{:S(2)}) copy-start(s32[32]{0:T(128)} %param.16) | copy-start | bytes 388
  172.8 1.0 copy-start.3
  178.7 231.4 %copy-start.1 = (bf16[1,2,512,256]{3,2,1,0:T(8,128)(2,1)S(1)}, bf16[1,2,512,256]{3,2,1,0:T(8,128)(2,1)}, u32[]{:S(2)}) copy-start(bf16[1,2,512,256]{3,2,1,0:T(8,128)(2,1)} %param.18) | copy-start | bytes 1572868
  297.2 234.2 %copy-start.4 = (f32[1,16,512]{2,1,0:T(8,128)S(1)}, f32[1,16,512]{2,1,0:T(8,128)}, u32[]{:S(2)}) copy-start(f32[1,16,512]{2,1,0:T(8,128)} %param.12) | copy-start | bytes 98308
Sparse Core Ops, SparseCore 0:
  297.3 233.9 all-reduce.1
